TPU v7x, 32 devices: a whole 2x2x4 slice. The times are simulated.
32 devices in a mesh: node: 8 (over z, y), feat: 4 (over x, core).
Axes of the slice: x: 2, y: 2, z: 4, core: 2. Of those that a mesh axis runs over, the one named last changes fastest.
Arguments:
- features: bfloat16 [32768, 256], P(('node', 'feat')), may hold values from -6 to 6
- weight: bfloat16 [256, 256], replicated, may hold values from -1.5 to 1.5
- grad_out: bfloat16 [32768, 256], P(('node', 'feat')), may hold values from -6 to 6
- local_rows: int32 [8, 4, 32], P('node', 'feat'), may hold values from 0 to 7
- local_cols: int32 [8, 4, 32], P('node', 'feat'), may hold values from 0 to 31
- local_values: bfloat16 [8, 4, 32, 128, 128], P('node', 'feat'), may hold values from 0 to 3, as said below
- remote_rows: int32 [8, 4, 3, 16], P('node', 'feat'), may hold values from 0 to 7
- remote_slots: int32 [8, 4, 3, 16], P('node', 'feat'), may hold values from 0 to 15
- remote_values: bfloat16 [8, 4, 3, 16, 128, 128], P('node', 'feat'), may hold values from 0 to 3, as said below
- send_blocks: int32 [8, 3, 16], P('node'), may hold values from 0 to 31, as said below
- tile_counts: int32 [8, 4, 4], P('node', 'feat'), may hold values from 1 to 32, as said below
Outputs:
- output: bfloat16 [32768, 256], P(('node', 'feat'))
- grad_features: bfloat16 [32768, 256], P(('node', 'feat'))
Inputs may be any that keep to these rules, and one draw needn't show every extreme that they name: `tile_counts`: column 0 is at most 32 and every other column at most 16; each column reaches its bound on some device, and other devices hold all, a half or a quarter of it, at least 1. `send_blocks`: the 16 blocks of one part and round are distinct. `local_values`: each entry is zero or a positive edge weight. `remote_values`: each entry is zero or a positive edge weight.
All inputs are finite; a program needn't handle non-finite values.
Results may differ from a plain program's by a relative error of at most 0.0049.
Values may be sent and summed in bfloat16 or wider, within the bound.
A program may use at most 128 MiB of HBM per device.

v0:
```python
import jax
import jax.numpy as jnp
from jax import lax
from jax.sharding import PartitionSpec as P


def swapped(array, axis, apart):
    return lax.ppermute(array, axis, [(i, i ^ 1 << apart) for i in range(lax.axis_size(axis))])


def spread(one_hot, values):
    return jnp.einsum("tb,tif->bif", one_hot, values, precision=lax.Precision.HIGHEST)


def masked_hot(targets, width, live):
    target_ids = jnp.arange(width, dtype=jnp.int32)
    return ((targets[:, None] == target_ids[None, :]) & live[:, None]).astype(jnp.float32)


def body(
    features,
    weight,
    grad_out,
    local_rows,
    local_cols,
    local_values,
    remote_rows,
    remote_slots,
    remote_values,
    send_blocks,
    tile_counts,
):
    rows_dev, feat_cols = features.shape
    block_rows = local_values.shape[-1]
    own_count = rows_dev // block_rows
    rounds = send_blocks.shape[1]
    log_nodes = lax.axis_size("node").bit_length() - 1
    own_blocks = features.reshape(own_count, block_rows, feat_cols)
    gathered = lax.all_gather(features, "feat", axis=0, tiled=True)
    part_count = gathered.shape[0] // block_rows
    part_feats = gathered.reshape(part_count, block_rows, feat_cols)
    counts = tile_counts[0, 0]
    dests = local_rows[0, 0]
    sources_ids = local_cols[0, 0]
    local_vals = local_values[0, 0]
    local_live = jnp.arange(local_vals.shape[0], dtype=jnp.int32) < counts[0]
    local_hot = masked_hot(dests, own_count, local_live)
    local_prod = jnp.einsum(
        "tij,tjf->tif", local_vals, part_feats[sources_ids], preferred_element_type=jnp.float32
    )
    totals = own_blocks.astype(jnp.float32) + spread(local_hot, local_prod)
    rowsum = jnp.einsum(
        "tb,ti->bi",
        local_hot,
        jnp.sum(local_vals, axis=-1, dtype=jnp.float32),
        precision=lax.Precision.HIGHEST,
    )
    round_live = []
    for round_no in range(rounds):
        bit_no = round_no * log_nodes // rounds
        send_order = send_blocks[0, round_no]
        slots = remote_slots[0, 0, round_no]
        arrived = swapped(part_feats[send_order], "node", bit_no)
        sources = arrived[slots]
        remote_vals = remote_values[0, 0, round_no]
        remote_live = jnp.arange(remote_vals.shape[0], dtype=jnp.int32) < counts[round_no + 1]
        round_live.append(remote_live)
        remote_hot = masked_hot(remote_rows[0, 0, round_no], own_count, remote_live)
        remote_prod = jnp.einsum(
            "tij,tjf->tif", remote_vals, sources, preferred_element_type=jnp.float32
        )
        totals = totals + spread(remote_hot, remote_prod)
        rowsum = rowsum + jnp.einsum(
            "tb,ti->bi",
            remote_hot,
            jnp.sum(remote_vals, axis=-1, dtype=jnp.float32),
            precision=lax.Precision.HIGHEST,
        )
    degree = 1.0 + rowsum
    hidden = (totals / degree[:, :, None]).astype(jnp.bfloat16).reshape(rows_dev, feat_cols)
    degree_flat = degree.reshape(rows_dev)
    output = jnp.dot(hidden, weight, preferred_element_type=jnp.float32).astype(jnp.bfloat16)
    grad_dense = lax.dot_general(
        grad_out, weight, (((1,), (1,)), ((), ())), preferred_element_type=jnp.float32
    )
    grad_hidden = (grad_dense / degree_flat[:, None]).astype(jnp.bfloat16)
    grad_blocks = grad_hidden.reshape(own_count, block_rows, feat_cols)
    local_back = jnp.einsum(
        "tij,tif->tjf", local_vals, grad_blocks[dests], preferred_element_type=jnp.float32
    )
    part_acc = spread(masked_hot(sources_ids, part_count, local_live), local_back)
    for round_no in range(rounds):
        bit_no = round_no * log_nodes // rounds
        remote_vals = remote_values[0, 0, round_no]
        remote_live = round_live[round_no]
        remote_back = jnp.einsum(
            "tij,tif->tjf",
            remote_vals,
            grad_blocks[remote_rows[0, 0, round_no]],
            preferred_element_type=jnp.float32,
        )
        send_order = send_blocks[0, round_no]
        need_count = send_order.shape[0]
        parcel = spread(
            masked_hot(remote_slots[0, 0, round_no], need_count, remote_live), remote_back
        )
        returned = swapped(parcel, "node", bit_no)
        all_live = jnp.ones((need_count,), dtype=jnp.bool_)
        part_acc = part_acc + spread(masked_hot(send_order, part_count, all_live), returned)
    shares = lax.psum_scatter(
        part_acc.reshape(part_count * block_rows, feat_cols),
        "feat",
        scatter_dimension=0,
        tiled=True,
    )
    grad_features = (grad_hidden.astype(jnp.float32) + shares).astype(jnp.bfloat16)
    return (output, grad_features)


def solution(mesh):
    in_specs = (
        P(("node", "feat"), None),
        P(),
        P(("node", "feat"), None),
        P("node", "feat", None),
        P("node", "feat", None),
        P("node", "feat", None, None, None),
        P("node", "feat", None, None),
        P("node", "feat", None, None),
        P("node", "feat", None, None, None, None),
        P("node", None, None),
        P("node", "feat", None),
    )
    out_specs = (P(("node", "feat"), None), P(("node", "feat"), None))
    return jax.shard_map(body, mesh=mesh, in_specs=in_specs, out_specs=out_specs, check_vma=False)
```

profile of v0, /device:TPU:7, one launch (start us, length us, event | category | flops | bytes accessed | tf_op | source)
XLA Modules:
  0.0 247.7 jit_solution(13713868402113608686)
XLA Ops:
  9.4 1.5 fusion.130
  12.8 1.6 convert_reduce_fusion
  16.4 1.6 gather_fusion.9
  18.0 3.1 %convolution_bitcast_fusion.1 = f32[16,128,256]{1,2,0:T(8,128)} fusion(bf16[16,128,256]{2,1,0:T(8,128)(2,1)} %gather_fusion.9, bf16[1,1,3,16,128,128]{5,4,3,2,1,0:T(8,128)(2,1)S(1)} %copy-done.2), kind=kOutput, calls=%fused_computation.24 | convolution fusion | flops 134217728 | bytes 3670016 | tf_op jit(solution)/shard_map/tij,tif->tjf/dot_general | solution.py:96
  21.1 3.1 %copy.25 = f32[16,128,256]{2,0,1:T(8,128)} copy(f32[16,128,256]{1,2,0:T(8,128)} %convolution_bitcast_fusion.1) | data formatting | bytes 4194304 | tf_op jit(solution)/shard_map/tij,tif->tjf/dot_general | solution.py:96
  24.2 4.1 %fusion.65 = f32[16,128,256]{2,0,1:T(8,128)} fusion(f32[16,128,256]{2,0,1:T(8,128)} %copy.25, s32[16]{0:T(128)S(1)} %get-tuple-element.10, pred[16]{0:T(512)(128)(4,1)S(1)} %iota_compare_fusion.12), kind=kOutput, calls=%fused_computation.81 | convolution fusion | flops 100663808 | bytes 4194384 | tf_op jit(solution)/shard_map/tb,tif->bif/dot_general | solution.py:12
  28.3 1.3 collective-permute-start.4
  29.6 1.6 gather_fusion.8
  31.1 3.1 %convolution_bitcast_fusion.2 = f32[16,128,256]{1,2,0:T(8,128)} fusion(bf16[16,128,256]{2,1,0:T(8,128)(2,1)} %gather_fusion.8, bf16[1,1,3,16,128,128]{5,4,3,2,1,0:T(8,128)(2,1)S(1)} %copy-done.2), kind=kOutput, calls=%fused_computation.25 | convolution fusion | flops 134217728 | bytes 3670016 | tf_op jit(solution)/shard_map/tij,tif->tjf/dot_general | solution.py:96
  34.2 3.1 %copy.24 = f32[16,128,256]{2,0,1:T(8,128)} copy(f32[16,128,256]{1,2,0:T(8,128)} %convolution_bitcast_fusion.2) | data formatting | bytes 4194304 | tf_op jit(solution)/shard_map/tij,tif->tjf/dot_general | solution.py:96
  37.3 4.1 %fusion.58 = f32[16,128,256]{2,0,1:T(8,128)} fusion(f32[16,128,256]{2,0,1:T(8,128)} %copy.24, s32[16]{0:T(128)S(1)} %get-tuple-element.9, pred[16]{0:T(512)(128)(4,1)S(1)} %iota_compare_fusion.13), kind=kOutput, calls=%fused_computation.76 | convolution fusion | flops 100663808 | bytes 4194384 | tf_op jit(solution)/shard_map/tb,tif->bif/dot_general | solution.py:12
  41.6 1.6 gather_fusion.10
  43.2 3.0 %convolution_bitcast_fusion = f32[16,128,256]{1,2,0:T(8,128)} fusion(bf16[16,128,256]{2,1,0:T(8,128)(2,1)} %gather_fusion.10, bf16[1,1,3,16,128,128]{5,4,3,2,1,0:T(8,128)(2,1)S(1)} %copy-done.2), kind=kOutput, calls=%fused_computation.23 | convolution fusion | flops 134217728 | bytes 3670016 | tf_op jit(solution)/shard_map/tij,tif->tjf/dot_general | solution.py:96
  46.2 3.1 %copy.26 = f32[16,128,256]{2,0,1:T(8,128)} copy(f32[16,128,256]{1,2,0:T(8,128)} %convolution_bitcast_fusion) | data formatting | bytes 4194304 | tf_op jit(solution)/shard_map/tij,tif->tjf/dot_general | solution.py:96
  49.3 4.1 %fusion.74 = f32[16,128,256]{2,0,1:T(8,128)} fusion(f32[16,128,256]{2,0,1:T(8,128)} %copy.26, s32[16]{0:T(128)S(1)} %get-tuple-element.8, pred[16]{0:T(512)(128)(4,1)S(1)} %iota_compare_fusion.11), kind=kOutput, calls=%fused_computation.86 | convolution fusion | flops 100663808 | bytes 4194384 | tf_op jit(solution)/shard_map/tb,tif->bif/dot_general | solution.py:12
  53.4 2.3 collective-permute-start.5
  55.7 2.0 gather_fusion.7
  57.7 4.6 %fusion.30 = f32[32,256,128]{2,1,0:T(8,128)} fusion(bf16[32,128,256]{2,1,0:T(8,128)(2,1)} %gather_fusion.7, bf16[1,1,32,128,128]{4,3,2,1,0:T(8,128)(2,1)} %param.16), kind=kOutput, calls=%fused_computation.39 | convolution fusion | flops 268435456 | bytes 7340032 | tf_op jit(solution)/shard_map/tij,tif->tjf/dot_general | solution.py:88
  62.3 5.5 %copy.23 = f32[32,256,128]{1,0,2:T(8,128)} copy(f32[32,256,128]{2,1,0:T(8,128)} %fusion.30) | data formatting | bytes 8388608 | tf_op jit(solution)/shard_map/tij,tif->tjf/dot_general | solution.py:88
  67.8 4.4 %fusion = f32[32,128,256]{2,0,1:T(8,128)S(1)} fusion(f32[32,256,128]{1,0,2:T(8,128)} %copy.23, s32[32]{0:T(128)S(1)} %bitcast.203, pred[32]{0:T(512)(128)(4,1)S(1)} %iota_compare_fusion.14), kind=kOutput, calls=%fused_computation.11 | convolution fusion | flops 402655232 | bytes 8388768 | tf_op jit(solution)/shard_map/tb,tif->bif/dot_general | solution.py:12
  72.2 23.9 %collective-permute-done.4 = f32[16,128,256]{2,0,1:T(8,128)} collective-permute-done((f32[16,128,256]{2,0,1:T(8,128)}, f32[16,128,256]{2,0,1:T(8,128)}, u32[]{:S(2)}, u32[]{:S(2)}) %collective-permute-start.4) | collective-permute-done | bytes 2097184 | tf_op jit(solution)/shard_map/ppermute | solution.py:8
  96.1 3.5 %fusion.61 = f32[32,128,256]{2,0,1:T(8,128)S(1)} fusion(f32[16,128,256]{2,0,1:T(8,128)} %collective-permute-done.4, s32[16]{0:T(128)S(1)} %get-tuple-element.7), kind=kOutput, calls=%fused_computation.78 | convolution fusion | flops 201327104 | bytes 6291520 | tf_op jit(solution)/shard_map/tb,tif->bif/dot_general | solution.py:12
  99.7 3.5 %fusion.54 = f32[32,128,256]{2,0,1:T(8,128)S(1)} fusion(f32[16,128,256]{2,0,1:T(8,128)} %collective-permute-done.3, s32[16]{0:T(128)S(1)} %get-tuple-element.6), kind=kOutput, calls=%fused_computation.73 | convolution fusion | flops 201327104 | bytes 6291520 | tf_op jit(solution)/shard_map/tb,tif->bif/dot_general | solution.py:12
  103.2 42.4 %collective-permute-done.5 = f32[16,128,256]{2,0,1:T(8,128)} collective-permute-done((f32[16,128,256]{2,0,1:T(8,128)}, f32[16,128,256]{2,0,1:T(8,128)}, u32[]{:S(2)}, u32[]{:S(2)}) %collective-permute-start.5) | collective-permute-done | bytes 2097184 | tf_op jit(solution)/shard_map/ppermute | solution.py:8
  145.6 4.4 %add_add_fusion = f32[32,128,256]{2,0,1:T(8,128)S(1)} fusion(f32[32,128,256]{2,0,1:T(8,128)S(1)} %fusion.61, f32[32,128,256]{2,0,1:T(8,128)S(1)} %fusion, f32[32,128,256]{2,0,1:T(8,128)S(1)} %fusion.54, f32[16,128,256]{2,0,1:T(8,128)} %collective-permute-done.5, s32[16]{0:T(128)S(1)} %get-tuple-element.5), kind=kOutput, calls=%fused_computation.15 | convolution fusion | flops 204472832 | bytes 18874432 | tf_op jit(solution)/shard_map/tb,tif->bif/dot_general | solution.py:12
  150.0 4.4 %copy.18 = f32[32,128,256]{2,1,0:T(8,128)} copy(f32[32,128,256]{2,0,1:T(8,128)S(1)} %add_add_fusion) | data formatting | bytes 8388608 | tf_op jit(solution)/shard_map/add | solution.py:109
  154.5 3.2 %gather_fusion.5 = bf16[16,128,256]{2,1,0:T(8,128)(2,1)} fusion(bf16[32,128,256]{2,1,0:T(8,128)(2,1)} %bitcast.194, s32[1024]{0:T(1024)S(1)} %pad_clamp_fusion.5), kind=kCustom, calls=%fused_computation.5 | custom fusion | bytes 2097216 | tf_op jit(solution)/shard_map/gather | solution.py:63
  157.8 1.1 convert.1
  159.0 3.2 %gather_fusion.3 = bf16[16,128,256]{2,1,0:T(8,128)(2,1)} fusion(bf16[32,128,256]{2,1,0:T(8,128)(2,1)} %bitcast.195, s32[1024]{0:T(1024)S(1)} %pad_clamp_fusion.7), kind=kCustom, calls=%fused_computation.3 | custom fusion | bytes 2097216 | tf_op jit(solution)/shard_map/gather | solution.py:63
  162.2 2.4 collective-permute-start.1
  164.6 4.1 %gather_fusion = bf16[32,128,256]{2,1,0:T(8,128)(2,1)} fusion(bf16[32,128,256]{2,1,0:T(8,128)(2,1)} %bitcast.196, s32[1024]{0:T(1024)S(1)} %pad_clamp_fusion.10), kind=kCustom, calls=%fused_computation | custom fusion | bytes 4194432 | tf_op jit(solution)/shard_map/gather | solution.py:49
  168.7 3.2 %gather_fusion.1 = bf16[16,128,256]{2,1,0:T(8,128)(2,1)} fusion(bf16[32,128,256]{2,1,0:T(8,128)(2,1)} %bitcast.197, s32[1024]{0:T(1024)S(1)} %pad_clamp_fusion.9), kind=kCustom, calls=%fused_computation.1 | custom fusion | bytes 2097216 | tf_op jit(solution)/shard_map/gather | solution.py:63
  171.9 1.4 collective-permute-start
  173.3 4.8 %fusion.32 = f32[32,256,128]{2,1,0:T(8,128)} fusion(bf16[32,128,256]{2,1,0:T(8,128)(2,1)} %gather_fusion, bf16[1,1,32,128,128]{4,3,2,1,0:T(8,128)(2,1)} %param.16), kind=kOutput, calls=%fused_computation.41 | convolution fusion | flops 268435456 | bytes 7340032 | tf_op jit(solution)/shard_map/tij,tjf->tif/dot_general | solution.py:48
  178.1 5.5 %copy.19 = f32[32,256,128]{1,0,2:T(8,128)} copy(f32[32,256,128]{2,1,0:T(8,128)} %fusion.32) | data formatting | bytes 8388608 | tf_op jit(solution)/shard_map/tij,tjf->tif/dot_general | solution.py:48
  183.6 5.4 %fusion.22 = f32[8,128,256]{2,0,1:T(8,128)} fusion(f32[32,256,128]{1,0,2:T(8,128)} %copy.19, f32[8,128,256]{2,1,0:T(8,128)} %convert.1, s32[32]{0:T(128)S(1)} %bitcast.202, pred[32]{0:T(512)(128)(4,1)S(1)} %iota_compare_fusion.14), kind=kOutput, calls=%fused_computation.30 | convolution fusion | flops 100925952 | bytes 6291616 | tf_op jit(solution)/shard_map/tb,tif->bif/dot_general | solution.py:12
  189.0 17.3 %collective-permute-done.2 = bf16[16,128,256]{2,1,0:T(8,128)(2,1)} collective-permute-done((bf16[16,128,256]{2,1,0:T(8,128)(2,1)}, bf16[16,128,256]{2,1,0:T(8,128)(2,1)}, u32[]{:S(2)}, u32[]{:S(2)}) %collective-permute-start.2) | collective-permute-done | bytes 1048608 | tf_op jit(solution)/shard_map/ppermute | solution.py:8
  206.3 2.8 %gather_fusion.6 = bf16[16,128,256]{2,1,0:T(8,128)(2,1)} fusion(bf16[16,128,256]{2,1,0:T(8,128)(2,1)} %collective-permute-done.2, s32[1024]{0:T(1024)S(1)} %pad_clamp_fusion.4), kind=kCustom, calls=%fused_computation.6 | custom fusion | bytes 2097216 | tf_op jit(solution)/shard_map/gather | solution.py:64
  209.2 3.1 %fusion.35 = f32[16,256,128]{2,1,0:T(8,128)} fusion(bf16[16,128,256]{2,1,0:T(8,128)(2,1)} %gather_fusion.6, bf16[1,1,3,16,128,128]{5,4,3,2,1,0:T(8,128)(2,1)S(1)} %copy-done.2), kind=kOutput, calls=%fused_computation.48 | convolution fusion | flops 134217728 | bytes 3670016 | tf_op jit(solution)/shard_map/tij,tjf->tif/dot_general | solution.py:69
  212.2 3.2 %copy.22 = f32[16,256,128]{1,0,2:T(8,128)} copy(f32[16,256,128]{2,1,0:T(8,128)} %fusion.35) | data formatting | bytes 4194304 | tf_op jit(solution)/shard_map/tij,tjf->tif/dot_general | solution.py:69
  215.4 2.8 %gather_fusion.4 = bf16[16,128,256]{2,1,0:T(8,128)(2,1)} fusion(bf16[16,128,256]{2,1,0:T(8,128)(2,1)} %collective-permute-done.1, s32[1024]{0:T(1024)S(1)} %pad_clamp_fusion.6), kind=kCustom, calls=%fused_computation.4 | custom fusion | bytes 2097216 | tf_op jit(solution)/shard_map/gather | solution.py:64
  218.2 3.1 %fusion.38 = f32[16,256,128]{2,1,0:T(8,128)} fusion(bf16[16,128,256]{2,1,0:T(8,128)(2,1)} %gather_fusion.4, bf16[1,1,3,16,128,128]{5,4,3,2,1,0:T(8,128)(2,1)S(1)} %copy-done.2), kind=kOutput, calls=%fused_computation.51 | convolution fusion | flops 134217728 | bytes 3670016 | tf_op jit(solution)/shard_map/tij,tjf->tif/dot_general | solution.py:69
  221.3 3.1 %copy.21 = f32[16,256,128]{1,0,2:T(8,128)} copy(f32[16,256,128]{2,1,0:T(8,128)} %fusion.38) | data formatting | bytes 4194304 | tf_op jit(solution)/shard_map/tij,tjf->tif/dot_general | solution.py:69
  224.5 2.8 %gather_fusion.2 = bf16[16,128,256]{2,1,0:T(8,128)(2,1)} fusion(bf16[16,128,256]{2,1,0:T(8,128)(2,1)} %collective-permute-done, s32[1024]{0:T(1024)S(1)} %pad_clamp_fusion.8), kind=kCustom, calls=%fused_computation.2 | custom fusion | bytes 2097216 | tf_op jit(solution)/shard_map/gather | solution.py:64
  227.3 3.1 %fusion.41 = f32[16,256,128]{2,1,0:T(8,128)} fusion(bf16[16,128,256]{2,1,0:T(8,128)(2,1)} %gather_fusion.2, bf16[1,1,3,16,128,128]{5,4,3,2,1,0:T(8,128)(2,1)S(1)} %copy-done.2), kind=kOutput, calls=%fused_computation.54 | convolution fusion | flops 134217728 | bytes 3670016 | tf_op jit(solution)/shard_map/tij,tjf->tif/dot_general | solution.py:69
  230.4 2.2 copy.20
  232.6 2.6 %fusion.4 = f32[8,128,256]{2,0,1:T(8,128)S(1)} fusion(f32[16,256,128]{1,0,2:T(8,128)} %copy.22, s32[16]{0:T(128)S(1)} %get-tuple-element.15, pred[16]{0:T(512)(128)(4,1)S(1)} %iota_compare_fusion.11), kind=kOutput, calls=%fused_computation.16 | convolution fusion | flops 50331904 | bytes 3145808 | tf_op jit(solution)/shard_map/tb,tif->bif/dot_general | solution.py:12
  238.7 2.1 add_convert_fusion
  (66 shorter events, 10.1 us)
Async XLA Ops:
  7.2 8.9 %copy-start = (bf16[1024,256]{1,0:T(8,128)(2,1)S(1)}, bf16[1024,256]{1,0:T(8,128)(2,1)}, u32[]{:S(2)}) copy-start(bf16[1024,256]{1,0:T(8,128)(2,1)} %param.13) | copy-start | bytes 1572868
  7.2 7.2 %copy-start.2 = (bf16[1,1,3,16,128,128]{5,4,3,2,1,0:T(8,128)(2,1)S(1)}, bf16[1,1,3,16,128,128]{5,4,3,2,1,0:T(8,128)(2,1)}, u32[]{:S(2)}) copy-start(bf16[1,1,3,16,128,128]{5,4,3,2,1,0:T(8,128)(2,1)} %param.19) | copy-start | bytes 4718596
  7.2 8.3 %copy-start.9 = (s32[1,1,32]{2,1,0:T(1,128)S(1)}, s32[1,1,32]{2,1,0:T(1,128)}, u32[]{:S(2)}) copy-start(s32[1,1,32]{2,1,0:T(1,128)} %param.14) | copy-start | bytes 388
  7.2 8.8 %copy-start.6 = (bf16[256,256]{1,0:T(8,128)(2,1)S(1)}, bf16[256,256]{1,0:T(8,128)(2,1)}, u32[]{:S(2)}) copy-start(bf16[256,256]{1,0:T(8,128)(2,1)} %param.12) | copy-start | bytes 393220
  7.2 147.3 %all-gather.2.cloned.1.call-start = ((), (), s32[]{:S(2)}) async-start(), calls=%async_computation.1 | async-start | bytes 2621440 | tf_op jit(solution)/shard_map/all_gather | solution.py:39
  7.9 230.8 %reduce-scatter.2.cloned.1.call-start = ((), (), s32[]{:S(2)}) async-start(), calls=%async_computation.2 | async-start | bytes 5242880 | tf_op jit(solution)/shard_map/reduce_scatter | solution.py:110
  21.1 3.1 %copy-start.8 = (s32[1,1,3,16]{3,1,2,0:T(1,128)S(1)}, s32[1,1,3,16]{3,1,2,0:T(1,128)}, u32[]{:S(2)}) copy-start(s32[1,1,3,16]{3,1,2,0:T(1,128)} %param.18) | copy-start | bytes 580
  28.3 67.9 %collective-permute-start.4 = (f32[16,128,256]{2,0,1:T(8,128)}, f32[16,128,256]{2,0,1:T(8,128)}, u32[]{:S(2)}, u32[]{:S(2)}) collective-permute-start(f32[16,128,256]{2,0,1:T(8,128)} %fusion.65), channel_id=1, source_target_pairs={{0,8},{4,12},{8,0},{12,4},{16,24},{20,28},{24,16},{28,20},{1,9},{5... | collective-permute-start | bytes 6291464 | tf_op jit(solution)/shard_map/ppermute | solution.py:8
  41.4 58.3 %collective-permute-start.3 = (f32[16,128,256]{2,0,1:T(8,128)}, f32[16,128,256]{2,0,1:T(8,128)}, u32[]{:S(2)}, u32[]{:S(2)}) collective-permute-start(f32[16,128,256]{2,0,1:T(8,128)} %fusion.58), channel_id=1, source_target_pairs={{0,4},{4,0},{8,12},{12,8},{16,20},{20,16},{24,28},{28,24},{1,5},{5... | collective-permute-start | bytes 6291464 | tf_op jit(solution)/shard_map/ppermute | solution.py:8
  53.4 92.2 %collective-permute-start.5 = (f32[16,128,256]{2,0,1:T(8,128)}, f32[16,128,256]{2,0,1:T(8,128)}, u32[]{:S(2)}, u32[]{:S(2)}) collective-permute-start(f32[16,128,256]{2,0,1:T(8,128)} %fusion.74), channel_id=1, source_target_pairs={{0,16},{4,20},{8,24},{12,28},{16,0},{20,4},{24,8},{28,12},{1,17},{... | collective-permute-start | bytes 6291464 | tf_op jit(solution)/shard_map/ppermute | solution.py:8
  62.3 5.5 %copy-start.7 = (s32[1,3,16]{2,0,1:T(1,128)S(1)}, s32[1,3,16]{2,0,1:T(1,128)}, u32[]{:S(2)}) copy-start(s32[1,3,16]{2,0,1:T(1,128)} %param.20) | copy-start | bytes 580
  62.3 5.5 %copy-start.10 = (s32[1,1,32]{2,1,0:T(1,128)S(1)}, s32[1,1,32]{2,1,0:T(1,128)}, u32[]{:S(2)}) copy-start(s32[1,1,32]{2,1,0:T(1,128)} %param.15) | copy-start | bytes 388
  154.4 3.5 %copy-start.5 = (bf16[1024,256]{1,0:T(8,128)(2,1)S(1)}, bf16[1024,256]{1,0:T(8,128)(2,1)}, u32[]{:S(2)}) copy-start(bf16[1024,256]{1,0:T(8,128)(2,1)} %param.11) | copy-start | bytes 1572868
  157.7 48.6 %collective-permute-start.2 = (bf16[16,128,256]{2,1,0:T(8,128)(2,1)}, bf16[16,128,256]{2,1,0:T(8,128)(2,1)}, u32[]{:S(2)}, u32[]{:S(2)}) collective-permute-start(bf16[16,128,256]{2,1,0:T(8,128)(2,1)} %gather_fusion.5), channel_id=1, source_target_pairs={{0,16},{4,20},{8,24},{12,28},{16,0},{20,4},{24,8},{28,12},{1,17},{... | collective-permute-start | bytes 3145736 | tf_op jit(solution)/shard_map/ppermute | solution.py:8
  162.2 53.2 %collective-permute-start.1 = (bf16[16,128,256]{2,1,0:T(8,128)(2,1)}, bf16[16,128,256]{2,1,0:T(8,128)(2,1)}, u32[]{:S(2)}, u32[]{:S(2)}) collective-permute-start(bf16[16,128,256]{2,1,0:T(8,128)(2,1)} %gather_fusion.3), channel_id=1, source_target_pairs={{0,8},{4,12},{8,0},{12,4},{16,24},{20,28},{24,16},{28,20},{1,9},{5... | collective-permute-start | bytes 3145736 | tf_op jit(solution)/shard_map/ppermute | solution.py:8
  171.9 52.6 %collective-permute-start = (bf16[16,128,256]{2,1,0:T(8,128)(2,1)}, bf16[16,128,256]{2,1,0:T(8,128)(2,1)}, u32[]{:S(2)}, u32[]{:S(2)}) collective-permute-start(bf16[16,128,256]{2,1,0:T(8,128)(2,1)} %gather_fusion.1), channel_id=1, source_target_pairs={{0,4},{4,0},{8,12},{12,8},{16,20},{20,16},{24,28},{28,24},{1,5},{5... | collective-permute-start | bytes 3145736 | tf_op jit(solution)/shard_map/ppermute | solution.py:8
  232.6 2.6 %copy-start.3 = (f32[16,256,128]{1,0,2:T(8,128)S(1)}, f32[16,256,128]{1,0,2:T(8,128)}, u32[]{:S(2)}) copy-start(f32[16,256,128]{1,0,2:T(8,128)} %copy.21) | copy-start | bytes 6291460
  235.2 1.2 copy-start.4
  236.4 4.4 %copy-start.1 = (bf16[1024,256]{1,0:T(8,128)(2,1)S(1)}, bf16[1024,256]{1,0:T(8,128)(2,1)}, u32[]{:S(2)}) copy-start(bf16[1024,256]{1,0:T(8,128)(2,1)} %param.13) | copy-start | bytes 1572868
Sparse Core Ops, SparseCore 0:
  9.6 23.2 all-gather.1
  154.5 45.0 reduce-scatter.1
where the time goes:
time: 251 us; the launch traced here: 248 us
  waiting for transfers between devices  84.4 us (34%)
  matrix products  67.8 us (27%)
  local copies, waits for them, and re-layouts  64.9 us (26%)
  between operations  14.4 us (6%)
  other arithmetic  8.61 us (3%)
  starting transfers between devices  7.71 us (3%)
    ppermute x6, waiting for transfers between devices, swapped(): lax.ppermute(array, axis, [(i, i ^ 1 << apart) for i in range(lax.axis_si...  83.7 us
    dot_general x11, matrix products, spread(): jnp.einsum('tb,tif->bif', one_hot, values, precision=lax.Precision.HIGHEST)  38 us
    gather x3, local copies, waits for them, and re-layouts, body(): arrived = swapped(part_feats[send_order], 'node', bit_no)  9.55 us
    dot_general x3, matrix products, body(): jnp.einsum('tij,tif->tjf', remote_vals, grad_blocks[remote_rows[0, 0, rou...  9.23 us
    dot_general x3, matrix products, body(): jnp.einsum('tij,tjf->tif', remote_vals, sources, preferred_element_type=j...  9.23 us
    dot_general x3, local copies, waits for them, and re-layouts, body(): jnp.einsum('tij,tif->tjf', remote_vals, grad_blocks[remote_rows[0, 0, rou...  9.22 us
    dot_general x3, local copies, waits for them, and re-layouts, body(): jnp.einsum('tij,tjf->tif', remote_vals, sources, preferred_element_type=j...  8.53 us
    gather x3, local copies, waits for them, and re-layouts, body(): sources = arrived[slots]  8.53 us
  transfers between devices with their start and end apart: 8, of which 3 were waited for; matrix products, arithmetic and copies ran while one was open for 56% of the time, Pallas kernels for 0%

commit v1 on v0

v1 whole, which is shorter than its diff:
```python
import functools

import jax
import jax.numpy as jnp
from jax import lax
from jax.experimental import pallas as pl
from jax.experimental.pallas import tpu as pltpu
from jax.sharding import PartitionSpec as P

F32 = jnp.float32
BF16 = jnp.bfloat16
VMEM_LIMIT = 56 * 2**20
GROUP = 8


def dot(a, b):
    return jnp.dot(a, b, preferred_element_type=F32)


def dot_tn(a, b):
    return lax.dot_general(a, b, (((0,), (0,)), ((), ())), preferred_element_type=F32)


def dot_nt(a, b):
    return lax.dot_general(a, b, (((1,), (1,)), ((), ())), preferred_element_type=F32)


def grouped(slots, step):
    group = min(GROUP, slots)
    assert slots % group == 0

    @pl.loop(0, slots // group)
    def _(g):
        step([g * group + u for u in range(group)])


def backward_kernel(
    grad_out,
    weight,
    local_rows,
    local_cols,
    local_values,
    remote_rows,
    remote_slots,
    remote_values,
    send_blocks,
    counts,
    acc,
    parcel,
    grad_hidden,
    degree,
    place,
    parcel_sum,
    degree_sum,
):
    block = local_values.shape[-1]
    own = grad_out.shape[0] // block
    part = acc.shape[0] - 1
    rounds, need = send_blocks.shape[1:]
    feat = grad_out.shape[1]
    for r in range(rounds):

        @pl.loop(0, part)
        def _(b):
            place[r, b] = -1

        @pl.loop(0, need)
        def _(i):
            place[r, send_blocks[0, r, i]] = i

    ones = jnp.ones((block, block), BF16)
    degree_sum[...] = jnp.ones_like(degree_sum)
    acc[...] = jnp.zeros_like(acc)
    parcel_sum[...] = jnp.zeros_like(parcel_sum)

    def local_degree(ts):
        sums = [dot(local_values[0, 0, t], ones) for t in ts]
        for t, s in zip(ts, sums):
            to = jnp.where(t < counts[0, 0, 0], local_rows[0, 0, t], own)
            degree_sum[to] += s

    grouped(local_values.shape[2], local_degree)
    for r in range(rounds):

        def remote_degree(ts):
            sums = [dot(remote_values[0, 0, r, t], ones) for t in ts]
            for t, s in zip(ts, sums):
                to = jnp.where(t < counts[0, 0, r + 1], remote_rows[0, 0, r, t], own)
                degree_sum[to] += s

        grouped(remote_values.shape[3], remote_degree)

    for d in range(own):
        rows = pl.ds(d * block, block)
        deg = degree_sum[d]
        degree[d] = deg
        dense = dot_nt(grad_out[rows, :], weight[...])
        wide = jnp.concatenate([deg] * (feat // block), axis=1)
        grad_hidden[d] = (dense / wide).astype(BF16)

    for r in range(rounds):

        def remote_back(ts):
            prods = [
                dot_tn(remote_values[0, 0, r, t], grad_hidden[remote_rows[0, 0, r, t]])
                for t in ts
            ]
            for t, p in zip(ts, prods):
                to = jnp.where(t < counts[0, 0, r + 1], remote_slots[0, 0, r, t], need)
                parcel_sum[r, to] += p

        grouped(remote_values.shape[3], remote_back)
        parcel[r] = parcel_sum[r, :need].astype(BF16)

    def local_back(ts):
        prods = [dot_tn(local_values[0, 0, t], grad_hidden[local_rows[0, 0, t]]) for t in ts]
        for t, p in zip(ts, prods):
            to = jnp.where(t < counts[0, 0, 0], local_cols[0, 0, t], part)
            acc[to] += p

    grouped(local_values.shape[2], local_back)


def forward_kernel(
    features,
    weight,
    local_rows,
    local_cols,
    local_values,
    remote_rows,
    remote_slots,
    remote_values,
    counts,
    degree,
    part_feats,
    arrived,
    output,
    totals,
):
    block = local_values.shape[-1]
    own = features.shape[0] // block
    rounds = remote_values.shape[2]
    feat = features.shape[1]
    for d in range(own):
        totals[d] = features[pl.ds(d * block, block), :].astype(F32)
    totals[own] = jnp.zeros_like(totals[own])

    def local_step(ts):
        prods = [dot(local_values[0, 0, t], part_feats[local_cols[0, 0, t]]) for t in ts]
        for t, p in zip(ts, prods):
            to = jnp.where(t < counts[0, 0, 0], local_rows[0, 0, t], own)
            totals[to] += p

    grouped(local_values.shape[2], local_step)
    for r in range(rounds):

        def remote_step(ts):
            prods = [
                dot(remote_values[0, 0, r, t], arrived[r, remote_slots[0, 0, r, t]]) for t in ts
            ]
            for t, p in zip(ts, prods):
                to = jnp.where(t < counts[0, 0, r + 1], remote_rows[0, 0, r, t], own)
                totals[to] += p

        grouped(remote_values.shape[3], remote_step)
    for d in range(own):
        wide = jnp.concatenate([degree[d]] * (feat // block), axis=1)
        hidden = (totals[d] / wide).astype(BF16)
        output[pl.ds(d * block, block), :] = dot(hidden, weight[...]).astype(BF16)


def exchange_kernel(
    bits,
    feat_size,
    features,
    send_blocks,
    place,
    acc,
    parcel,
    grad_hidden,
    part_feats,
    arrived,
    grad_features,
    send_buf,
    mate_parcel,
    parcel_out,
    returned,
    pair_out,
    pair_in,
    kept,
    cross_out,
    cross_in,
    feat_send,
    feat_recv,
    node_send,
    node_recv,
    pass_send,
    pass_recv,
    parcel_send,
    parcel_recv,
    back_send,
    back_recv,
    red_send,
    red_recv,
):
    rounds = len(bits)
    own, block, _ = grad_hidden.shape
    need = parcel.shape[1]
    half = need // 2
    node, f = lax.axis_index("node"), lax.axis_index("feat")
    h = lax.rem(f, 2)
    mate_h = 1 - h
    mate = f + 1 - 2 * h
    opp = lax.rem(f + 2, feat_size)
    partners = [node + (1 << b) * (1 - 2 * lax.rem(node // (1 << b), 2)) for b in bits]
    to_mate, to_opp = (node, mate), (node, opp)
    to_node = [(p, f) for p in partners]

    def remote(src, dst, send_sem, recv_sem, to):
        copy = pltpu.make_async_remote_copy(
            src_ref=src,
            dst_ref=dst,
            send_sem=send_sem,
            recv_sem=recv_sem,
            device_id=to,
            device_id_type=pl.DeviceIdType.MESH,
        )
        return copy

    barrier = pltpu.get_barrier_semaphore()
    for to in (to_mate, to_opp, *to_node):
        pl.semaphore_signal(barrier, inc=1, device_id=to, device_id_type=pl.DeviceIdType.MESH)
    pl.semaphore_wait(barrier, 2 + rounds)

    mine = part_feats.at[pl.ds(f * own, own)]
    for b in range(own):
        part_feats[f * own + b] = features[pl.ds(b * block, block), :]
    cross = remote(mine, mine, feat_send.at[0], feat_recv.at[0], to_opp)
    cross.start()
    pair = remote(mine, mine, feat_send.at[1], feat_recv.at[1], to_mate)
    pair.start()
    order = list(range(rounds))[::-1]
    swaps = [None] * rounds
    for r in order:
        swaps[r] = remote(
            parcel.at[r, pl.ds(mate_h * half, half)],
            mate_parcel.at[r],
            parcel_send.at[r],
            parcel_recv.at[r],
            to_mate,
        )
        swaps[r].start()
    backs = [None] * rounds
    for r in order:
        swaps[r].wait()

        @pl.loop(0, half)
        def _(i):
            total = parcel[r, h * half + i].astype(F32) + mate_parcel[r, i].astype(F32)
            parcel_out[r, i] = total.astype(BF16)

        backs[r] = remote(
            parcel_out.at[r], returned.at[r], back_send.at[r], back_recv.at[r], to_node[r]
        )
        backs[r].start()

    cross.wait()
    theirs = part_feats.at[pl.ds(opp * own, own)]
    relay = remote(theirs, theirs, feat_send.at[2], feat_recv.at[2], to_mate)
    relay.start()
    pair.wait()
    relay.wait()
    outs = [None] * rounds
    for r in order:

        @pl.loop(0, half)
        def _(i):
            send_buf[r, i] = part_feats[send_blocks[0, r, h * half + i]]

        outs[r] = remote(
            send_buf.at[r],
            arrived.at[r, pl.ds(h * half, half)],
            node_send.at[r],
            node_recv.at[r],
            to_node[r],
        )
        outs[r].start()

    for r in order:
        backs[r].wait()

    def gathered_sum(b):
        total = acc[b]
        for r in range(rounds):
            at = place[r, b] - h * half
            there = jnp.logical_and(at >= 0, at < half)
            found = returned[r, jnp.clip(at, 0, half - 1)].astype(F32)
            total = total + jnp.where(there, found, 0.0)
        return total

    for o in range(feat_size // 2):

        @pl.loop(0, own)
        def _(j):
            pair_out[o, j] = gathered_sum((2 * o + mate_h) * own + j).astype(BF16)

    pair_red = remote(pair_out, pair_in, red_send.at[0], red_recv.at[0], to_mate)
    pair_red.start()
    for o in range(feat_size // 2):

        @pl.loop(0, own)
        def _(j):
            kept[o, j] = gathered_sum((2 * o + h) * own + j)

    pair_red.wait()

    @pl.loop(0, own)
    def _(j):
        o = opp // 2
        cross_out[j] = (kept[o, j] + pair_in[o, j].astype(F32)).astype(BF16)

    cross_red = remote(cross_out, cross_in, red_send.at[1], red_recv.at[1], to_opp)
    cross_red.start()
    passes = [None] * rounds
    for r in order[::-1]:
        outs[r].wait()
        piece = arrived.at[r, pl.ds(h * half, half)]
        passes[r] = remote(piece, piece, pass_send.at[r], pass_recv.at[r], to_mate)
        passes[r].start()
    cross_red.wait()
    for j in range(own):
        o = f // 2
        total = kept[o, j] + pair_in[o, j].astype(F32)
        total = total + cross_in[j].astype(F32) + grad_hidden[j].astype(F32)
        grad_features[pl.ds(j * block, block), :] = total.astype(BF16)
    for r in range(rounds):
        passes[r].wait()


def body(
    features,
    weight,
    grad_out,
    local_rows,
    local_cols,
    local_values,
    remote_rows,
    remote_slots,
    remote_values,
    send_blocks,
    tile_counts,
):
    rows_dev, feat = features.shape
    block = local_values.shape[-1]
    own = rows_dev // block
    rounds, need = send_blocks.shape[1:]
    feat_size = lax.axis_size("feat")
    part = own * feat_size
    log_nodes = lax.axis_size("node").bit_length() - 1
    bits = [r * log_nodes // rounds for r in range(rounds)]
    half = need // 2
    assert feat_size == 4
    vmem = pl.BlockSpec(memory_space=pltpu.VMEM)
    smem = pl.BlockSpec(memory_space=pltpu.SMEM)
    tile_flops = 2 * block * block * feat * (local_values.shape[2] + rounds * need)
    acc, parcel, grad_hidden, degree, place = pl.pallas_call(
        backward_kernel,
        out_shape=(
            jax.ShapeDtypeStruct((part + 1, block, feat), F32),
            jax.ShapeDtypeStruct((rounds, need, block, feat), BF16),
            jax.ShapeDtypeStruct((own, block, feat), BF16),
            jax.ShapeDtypeStruct((own, block, block), F32),
            jax.ShapeDtypeStruct((rounds, part), jnp.int32),
        ),
        in_specs=[vmem, vmem, smem, smem, vmem, smem, smem, vmem, smem, smem],
        out_specs=(vmem, vmem, vmem, vmem, smem),
        scratch_shapes=[
            pltpu.VMEM((rounds, need + 1, block, feat), F32),
            pltpu.VMEM((own + 1, block, block), F32),
        ],
        compiler_params=pltpu.CompilerParams(vmem_limit_bytes=VMEM_LIMIT),
        cost_estimate=pl.CostEstimate(
            flops=2 * tile_flops, bytes_accessed=12 * 2**20, transcendentals=0
        ),
        name="backward_products",
    )(
        grad_out,
        weight,
        local_rows,
        local_cols,
        local_values,
        remote_rows,
        remote_slots,
        remote_values,
        send_blocks,
        tile_counts,
    )
    dma = pltpu.SemaphoreType.DMA
    part_feats, arrived, grad_features = pl.pallas_call(
        functools.partial(exchange_kernel, bits, feat_size),
        out_shape=(
            jax.ShapeDtypeStruct((part, block, feat), BF16),
            jax.ShapeDtypeStruct((rounds, need, block, feat), BF16),
            jax.ShapeDtypeStruct((rows_dev, feat), BF16),
        ),
        in_specs=[vmem, smem, smem, vmem, vmem, vmem],
        out_specs=(vmem, vmem, vmem),
        scratch_shapes=[
            pltpu.VMEM((rounds, half, block, feat), BF16),
            pltpu.VMEM((rounds, half, block, feat), BF16),
            pltpu.VMEM((rounds, half, block, feat), BF16),
            pltpu.VMEM((rounds, half, block, feat), BF16),
            pltpu.VMEM((feat_size // 2, own, block, feat), BF16),
            pltpu.VMEM((feat_size // 2, own, block, feat), BF16),
            pltpu.VMEM((feat_size // 2, own, block, feat), F32),
            pltpu.VMEM((own, block, feat), BF16),
            pltpu.VMEM((own, block, feat), BF16),
            dma((3,)),
            dma((3,)),
            dma((rounds,)),
            dma((rounds,)),
            dma((rounds,)),
            dma((rounds,)),
            dma((rounds,)),
            dma((rounds,)),
            dma((rounds,)),
            dma((rounds,)),
            dma((2,)),
            dma((2,)),
        ],
        compiler_params=pltpu.CompilerParams(
            vmem_limit_bytes=VMEM_LIMIT, collective_id=0, has_side_effects=True
        ),
        cost_estimate=pl.CostEstimate(flops=0, bytes_accessed=20 * 2**20, transcendentals=0),
        name="exchange",
    )(features, send_blocks, place, acc, parcel, grad_hidden)
    output = pl.pallas_call(
        forward_kernel,
        out_shape=jax.ShapeDtypeStruct((rows_dev, feat), BF16),
        in_specs=[vmem, vmem, smem, smem, vmem, smem, smem, vmem, smem, vmem, vmem, vmem],
        out_specs=vmem,
        scratch_shapes=[pltpu.VMEM((own + 1, block, feat), F32)],
        compiler_params=pltpu.CompilerParams(vmem_limit_bytes=VMEM_LIMIT),
        cost_estimate=pl.CostEstimate(
            flops=tile_flops, bytes_accessed=10 * 2**20, transcendentals=0
        ),
        name="forward_products",
    )(
        features,
        weight,
        local_rows,
        local_cols,
        local_values,
        remote_rows,
        remote_slots,
        remote_values,
        tile_counts,
        degree,
        part_feats,
        arrived,
    )
    return (output, grad_features)


def solution(mesh):
    in_specs = (
        P(("node", "feat"), None),
        P(),
        P(("node", "feat"), None),
        P("node", "feat", None),
        P("node", "feat", None),
        P("node", "feat", None, None, None),
        P("node", "feat", None, None),
        P("node", "feat", None, None),
        P("node", "feat", None, None, None, None),
        P("node", None, None),
        P("node", "feat", None),
    )
    out_specs = (P(("node", "feat"), None), P(("node", "feat"), None))
    return jax.shard_map(body, mesh=mesh, in_specs=in_specs, out_specs=out_specs, check_vma=False)
```

time: 251 us -> 89.5 us (0.36); the launches traced: 248 us -> 89.3 us
  waiting for transfers between devices: 84.4 us -> 0 us
  Pallas kernels: 0 us -> 84.1 us
  matrix products: 67.8 us -> 0 us
  local copies, waits for them, and re-layouts: 64.9 us -> 4.58 us
  between operations: 14.4 us -> 0.66 us
  other arithmetic: 8.61 us -> 0 us
  starting transfers between devices: 7.71 us -> 0 us
    pallas_call x0 -> x3, Pallas kernels: none -> 84.1 us  [the longest x1 62.6 us: body(): pl.pallas_call(functools.partial(exchange_kernel, bits, feat_size), out_s...]
    ppermute x6 -> x0, waiting for transfers between devices: 83.7 us -> none  [swapped(): lax.ppermute(array, axis, [(i, i ^ 1 << apart) for i in range(lax.axis_si...]
    dot_general x25 -> x0, matrix products: 67.8 us -> none  [the longest x11 38 us: spread(): jnp.einsum('tb,tif->bif', one_hot, values, precision=lax.Precision.HIGHEST)]
    gather x11 -> x0, local copies, waits for them, and re-layouts: 29 us -> none  [the longest x3 9.55 us: body(): arrived = swapped(part_feats[send_order], 'node', bit_no)]
    dot_general x8 -> x0, local copies, waits for them, and re-layouts: 28.7 us -> none  [the longest x3 9.22 us: body(): jnp.einsum('tij,tif->tjf', remote_vals, grad_blocks[remote_rows[0, 0, rou...]
    ppermute x6 -> x0, starting transfers between devices: 7.63 us -> none  [swapped(): lax.ppermute(array, axis, [(i, i ^ 1 << apart) for i in range(lax.axis_si...]
    add x2 -> x0, local copies, waits for them, and re-layouts: 4.49 us -> none  [the longest x1 4.39 us: body(): part_acc + spread(masked_hot(send_order, part_count, all_live), returned)]
    unnamed x22 -> x6, local copies, waits for them, and re-layouts: 0.42 us -> 4.58 us
  transfers between devices with their start and end apart: 8 -> 0, of which waited for: 3 -> 0; matrix products, arithmetic and copies ran while one was open for 56% -> 0% of each run, Pallas kernels for 0% -> 0%
where the time goes in v1:
time: 89.5 us; the launch traced here: 89.3 us
  Pallas kernels  84.1 us (94%)
  local copies, waits for them, and re-layouts  4.58 us (5%)
    pallas_call x1, Pallas kernels, body(): pl.pallas_call(functools.partial(exchange_kernel, bits, feat_size), out_s...  62.6 us
    pallas_call x1, Pallas kernels, body(): pl.pallas_call(backward_kernel, out_shape=(jax.ShapeDtypeStruct((part + 1...  13.5 us
    pallas_call x1, Pallas kernels, body(): pl.pallas_call(forward_kernel, out_shape=jax.ShapeDtypeStruct((rows_dev,...  7.98 us
    unnamed x6, local copies, waits for them, and re-layouts  4.58 us

profile of v1, /device:TPU:7, one launch (start us, length us, event | category | flops | bytes accessed | tf_op | source)
XLA Modules:
  0.0 89.3 jit_solution(3160770201755186736)
XLA Ops:
  0.6 1.3 %copy.17.remote_rows = s32[1,1,3,16]{3,2,1,0:T(4,128)} copy(s32[1,1,3,16]{3,1,2,0:T(1,128)} %param.17) | data formatting | bytes 384 | tf_op args[6]
  1.9 1.3 %copy.18.remote_slots = s32[1,1,3,16]{3,2,1,0:T(4,128)} copy(s32[1,1,3,16]{3,1,2,0:T(1,128)} %param.18) | data formatting | bytes 384 | tf_op args[7]
  3.1 1.3 %copy.15.send_blocks = s32[1,3,16]{2,1,0:T(4,128)} copy(s32[1,3,16]{2,0,1:T(1,128)} %param.20) | data formatting | bytes 384 | tf_op args[9]
  4.4 13.5 %backward_products.1 = (f32[33,128,256]{2,1,0:T(8,128)}, bf16[3,16,128,256]{3,2,1,0:T(8,128)(2,1)}, bf16[8,128,256]{2,1,0:T(8,128)(2,1)}, f32[8,128,128]{2,1,0:T(8,128)}, s32[3,32]{1,0:T(4,128)}) custom-call(bf16[1024,256]{1,0:T(8,128)(2,1)} %grad_out.1, bf16[256,256]{1,0:T(8,128)(2,1)} %weight.3, s32[1,1,32]{2,1,0:T(1,128)} %local_rows.3, ...), custom_call_target="tpu_custom_call" | custom-call | flops 1342177280 | bytes 12582912 | tf_op jit(solution)/shard_map/backward_products/pallas_call | solution.py:366
  17.9 62.6 %exchange.1 = (bf16[32,128,256]{2,1,0:T(8,128)(2,1)}, bf16[3,16,128,256]{3,2,1,0:T(8,128)(2,1)}, bf16[1024,256]{1,0:T(8,128)(2,1)}) custom-call(bf16[1024,256]{1,0:T(8,128)(2,1)} %features.3, s32[1,3,16]{2,1,0:T(4,128)} %copy.15.send_blocks, s32[3,32]{1,0:T(4,128)} %get-tuple-element.11.place, f32[33,128,256]{2,1,0:T(8,128)} %get-tuple-element.12.acc, ...), custom_call_target="tpu_custom_call" | custom-call | bytes 20971520 | tf_op jit(solution)/shard_map/exchange/pallas_call | solution.py:399
  80.5 0.0 copy-start
  80.6 8.0 %forward_products.1 = bf16[1024,256]{1,0:T(8,128)(2,1)} custom-call(bf16[1024,256]{1,0:T(8,128)(2,1)} %features.3, bf16[256,256]{1,0:T(8,128)(2,1)} %weight.3, s32[1,1,32]{2,1,0:T(1,128)} %local_rows.3, s32[1,1,32]{2,1,0:T(1,128)} %local_cols.3, bf16[1,1,32,128,128]{4,3,2,1,0:T(8,128)(2,1)} %local_values.3, s32[1,1,3,16]{3,2,1,0:T(4,128)} %copy.17.remote_rows, ...), custom_call_target="tpu_custom_call" | custom-call | flops 671088640 | bytes 10485760 | tf_op jit(solution)/shard_map/forward_products/pallas_call | solution.py:437
  88.5 0.0 copy-done
  88.5 0.8 copy.20
Async XLA Ops:
  80.5 8.0 %copy-start = (bf16[1024,256]{1,0:T(8,128)(2,1)S(1)}, bf16[1024,256]{1,0:T(8,128)(2,1)}, u32[]{:S(2)}) copy-start(bf16[1024,256]{1,0:T(8,128)(2,1)} %get-tuple-element.21) | copy-start | bytes 1572868

commit v2 on v1

v2 whole, which is shorter than its diff:
```python
import functools

import jax
import jax.numpy as jnp
from jax import lax
from jax.experimental import pallas as pl
from jax.experimental.pallas import tpu as pltpu
from jax.sharding import PartitionSpec as P

F32 = jnp.float32
BF16 = jnp.bfloat16
VMEM_LIMIT = 56 * 2**20
GROUP = 8


def dot(a, b):
    return jnp.dot(a, b, preferred_element_type=F32)


def dot_tn(a, b):
    return lax.dot_general(a, b, (((0,), (0,)), ((), ())), preferred_element_type=F32)


def dot_nt(a, b):
    return lax.dot_general(a, b, (((1,), (1,)), ((), ())), preferred_element_type=F32)


def grouped(slots, step):
    group = min(GROUP, slots)
    assert slots % group == 0

    @pl.loop(0, slots // group)
    def _(g):
        step([g * group + u for u in range(group)])


class Layout:
    def __init__(self, slots, rounds, cap, need, own, part):
        self.slots, self.rounds, self.cap, self.need = slots, rounds, cap, need
        self.own, self.part = own, part
        sizes = (slots, slots, rounds * cap, rounds * cap, rounds * need, rounds + 1)
        starts = [sum(sizes[:i]) for i in range(len(sizes) + 1)]
        self.rows, self.cols, self.rrows, self.rslots, self.send, self.counts, _ = starts
        tiles = slots + rounds * cap
        sizes = (tiles, own, slots, part, rounds * cap, rounds * need, rounds * part)
        starts = [sum(sizes[:i]) for i in range(len(sizes) + 1)]
        self.prev_f, self.last_f, self.prev_l, self.last_l = starts[:4]
        self.prev_r, self.last_r, self.place, self.plan_size = starts[4:]
        self.tiles = tiles


def plan_kernel(
    lay, meta, grad_out, weight, local_values, remote_values, plan, grad_hidden, degree, degree_sum
):
    block = local_values.shape[-1]
    feat = grad_out.shape[1]

    @pl.loop(0, lay.plan_size)
    def _(i):
        plan[i] = -1

    @pl.loop(0, lay.slots)
    def _(t):
        @pl.when(t < meta[lay.counts])
        def _():
            d, c = meta[lay.rows + t], meta[lay.cols + t]
            plan[lay.prev_f + t] = plan[lay.last_f + d]
            plan[lay.last_f + d] = t
            plan[lay.prev_l + t] = plan[lay.last_l + c]
            plan[lay.last_l + c] = t

    for r in range(lay.rounds):

        @pl.loop(0, lay.cap)
        def _(t):
            at = r * lay.cap + t

            @pl.when(t < meta[lay.counts + r + 1])
            def _():
                d, c = meta[lay.rrows + at], meta[lay.rslots + at]
                plan[lay.prev_f + lay.slots + at] = plan[lay.last_f + d]
                plan[lay.last_f + d] = lay.slots + at
                plan[lay.prev_r + at] = plan[lay.last_r + r * lay.need + c]
                plan[lay.last_r + r * lay.need + c] = at

        @pl.loop(0, lay.need)
        def _(i):
            plan[lay.place + r * lay.part + meta[lay.send + r * lay.need + i]] = i

    ones = jnp.ones((block, block), BF16)
    degree_sum[...] = jnp.ones_like(degree_sum)

    def local_degree(ts):
        sums = [dot(local_values[0, 0, t], ones) for t in ts]
        for t, s in zip(ts, sums):
            to = jnp.where(t < meta[lay.counts], meta[lay.rows + t], lay.own)
            degree_sum[to] += s

    grouped(lay.slots, local_degree)
    for r in range(lay.rounds):

        def remote_degree(ts):
            sums = [dot(remote_values[0, 0, r, t], ones) for t in ts]
            for t, s in zip(ts, sums):
                live = t < meta[lay.counts + r + 1]
                to = jnp.where(live, meta[lay.rrows + r * lay.cap + t], lay.own)
                degree_sum[to] += s

        grouped(lay.cap, remote_degree)

    for d in range(lay.own):
        deg = degree_sum[d]
        degree[d] = deg
        dense = dot_nt(grad_out[pl.ds(d * block, block), :], weight[...])
        wide = jnp.concatenate([deg] * (feat // block), axis=1)
        grad_hidden[d] = (dense / wide).astype(BF16)


def exchange_kernel(
    lay,
    bits,
    feat_size,
    meta,
    plan,
    features,
    weight,
    local_values,
    remote_values,
    grad_hidden,
    degree,
    output,
    grad_features,
    part_feats,
    send_buf,
    mate_out,
    mate_parcel,
    parcel_out,
    returned,
    pair_out,
    pair_in,
    kept,
    cross_out,
    cross_in,
    sums_r,
    sums_l,
    sums_f,
    feat_send,
    feat_recv,
    node_send,
    node_recv,
    pass_send,
    pass_recv,
    parcel_send,
    parcel_recv,
    back_send,
    back_recv,
    red_send,
    red_recv,
    *arrived,
):
    rounds = len(bits)
    own, block, feat = grad_hidden.shape
    need, half = lay.need, lay.need // 2
    node, f = lax.axis_index("node"), lax.axis_index("feat")
    h = lax.rem(f, 2)
    mate_h = 1 - h
    mate = f + 1 - 2 * h
    opp = lax.rem(f + 2, feat_size)
    partners = [node + (1 << b) * (1 - 2 * lax.rem(node // (1 << b), 2)) for b in bits]
    to_mate, to_opp = (node, mate), (node, opp)
    to_node = [(p, f) for p in partners]

    def remote(src, dst, send_sem, recv_sem, to):
        return pltpu.make_async_remote_copy(
            src_ref=src,
            dst_ref=dst,
            send_sem=send_sem,
            recv_sem=recv_sem,
            device_id=to,
            device_id_type=pl.DeviceIdType.MESH,
        )

    barrier = pltpu.get_barrier_semaphore()
    for to in (to_mate, to_opp, *to_node):
        pl.semaphore_signal(barrier, inc=1, device_id=to, device_id_type=pl.DeviceIdType.MESH)
    pl.semaphore_wait(barrier, 2 + rounds)

    mine = part_feats.at[pl.ds(f * own, own)]
    for b in range(own):
        part_feats[f * own + b] = features[pl.ds(b * block, block), :]
    cross = remote(mine, mine, feat_send.at[0], feat_recv.at[0], to_opp)
    cross.start()
    pair = remote(mine, mine, feat_send.at[1], feat_recv.at[1], to_mate)
    pair.start()
    order = list(range(rounds))[::-1]

    def picked(sums, at):
        return jnp.where(at >= 0, sums[jnp.maximum(at, 0)], 0.0)

    def chain(sums, base, ts, prods, prev):
        for t, p in zip(ts, prods):
            sums[base + t] = p + picked(sums, plan[prev + t])

    def back_products(r):
        def step(ts):
            prods = [
                dot_tn(remote_values[0, 0, r, t], grad_hidden[meta[lay.rrows + r * lay.cap + t]])
                for t in ts
            ]
            chain(sums_r, r * lay.cap, ts, prods, lay.prev_r + r * lay.cap)

        grouped(lay.cap, step)

    def parcel(r, s):
        return picked(sums_r, plan[lay.last_r + r * need + s])

    swaps, backs = [None] * rounds, [None] * rounds

    def send_back(r):
        swaps[r].wait()

        @pl.loop(0, half)
        def _(i):
            total = parcel(r, h * half + i) + mate_parcel[r, i].astype(F32)
            parcel_out[r, i] = total.astype(BF16)

        backs[r] = remote(
            parcel_out.at[r], returned.at[r], back_send.at[r], back_recv.at[r], to_node[r]
        )
        backs[r].start()

    for k, r in enumerate(order):
        back_products(r)

        @pl.loop(0, half)
        def _(i):
            mate_out[r, i] = parcel(r, mate_h * half + i).astype(BF16)

        swaps[r] = remote(
            mate_out.at[r], mate_parcel.at[r], parcel_send.at[r], parcel_recv.at[r], to_mate
        )
        swaps[r].start()
        if k:
            send_back(order[k - 1])
    send_back(order[-1])

    cross.wait()
    theirs = part_feats.at[pl.ds(opp * own, own)]
    relay = remote(theirs, theirs, feat_send.at[2], feat_recv.at[2], to_mate)
    relay.start()
    pair.wait()
    relay.wait()
    outs = [None] * rounds
    for r in order:

        @pl.loop(0, half)
        def _(i):
            send_buf[r, i] = part_feats[meta[lay.send + r * need + h * half + i]]

        outs[r] = remote(
            send_buf.at[r],
            arrived[r].at[pl.ds(h * half, half)],
            node_send.at[r],
            node_recv.at[r],
            to_node[r],
        )
        outs[r].start()

    def local_back(ts):
        prods = [dot_tn(local_values[0, 0, t], grad_hidden[meta[lay.rows + t]]) for t in ts]
        chain(sums_l, 0, ts, prods, lay.prev_l)

    grouped(lay.slots, local_back)

    def local_forward(ts):
        prods = [dot(local_values[0, 0, t], part_feats[meta[lay.cols + t]]) for t in ts]
        chain(sums_f, 0, ts, prods, lay.prev_f)

    grouped(lay.slots, local_forward)

    for r in order[::-1]:
        backs[r].wait()

    def gathered_sum(b):
        total = picked(sums_l, plan[lay.last_l + b])
        for r in range(rounds):
            at = plan[lay.place + r * lay.part + b] - h * half
            there = jnp.logical_and(at >= 0, at < half)
            found = returned[r, jnp.clip(at, 0, half - 1)].astype(F32)
            total = total + jnp.where(there, found, 0.0)
        return total

    for o in range(feat_size // 2):

        @pl.loop(0, own)
        def _(j):
            pair_out[o, j] = gathered_sum((2 * o + mate_h) * own + j).astype(BF16)

    pair_red = remote(pair_out, pair_in, red_send.at[0], red_recv.at[0], to_mate)
    pair_red.start()
    for o in range(feat_size // 2):

        @pl.loop(0, own)
        def _(j):
            kept[o, j] = gathered_sum((2 * o + h) * own + j)

    pair_red.wait()

    @pl.loop(0, own)
    def _(j):
        o = opp // 2
        cross_out[j] = (kept[o, j] + pair_in[o, j].astype(F32)).astype(BF16)

    cross_red = remote(cross_out, cross_in, red_send.at[1], red_recv.at[1], to_opp)
    cross_red.start()
    passes = [None] * rounds

    def pass_on(r):
        outs[r].wait()
        piece = arrived[r].at[pl.ds(h * half, half)]
        passes[r] = remote(piece, piece, pass_send.at[r], pass_recv.at[r], to_mate)
        passes[r].start()

    def forward_products(r):
        passes[r].wait()

        def step(ts):
            prods = [
                dot(
                    remote_values[0, 0, r, t],
                    arrived[r][meta[lay.rslots + r * lay.cap + t]],
                )
                for t in ts
            ]
            base = lay.slots + r * lay.cap
            chain(sums_f, base, ts, prods, lay.prev_f + base)

        grouped(lay.cap, step)

    for r in range(rounds):
        pass_on(r)
        if r:
            forward_products(r - 1)
        if r == rounds - 2:
            cross_red.wait()
            for j in range(own):
                o = f // 2
                total = kept[o, j] + pair_in[o, j].astype(F32)
                total = total + cross_in[j].astype(F32) + grad_hidden[j].astype(F32)
                grad_features[pl.ds(j * block, block), :] = total.astype(BF16)
    forward_products(rounds - 1)
    for d in range(own):
        rows = pl.ds(d * block, block)
        total = features[rows, :].astype(F32) + picked(sums_f, plan[lay.last_f + d])
        wide = jnp.concatenate([degree[d]] * (feat // block), axis=1)
        hidden = (total / wide).astype(BF16)
        output[rows, :] = dot(hidden, weight[...]).astype(BF16)


def body(
    features,
    weight,
    grad_out,
    local_rows,
    local_cols,
    local_values,
    remote_rows,
    remote_slots,
    remote_values,
    send_blocks,
    tile_counts,
):
    rows_dev, feat = features.shape
    block = local_values.shape[-1]
    own = rows_dev // block
    rounds, need = send_blocks.shape[1:]
    feat_size = lax.axis_size("feat")
    part = own * feat_size
    log_nodes = lax.axis_size("node").bit_length() - 1
    bits = [r * log_nodes // rounds for r in range(rounds)]
    half = need // 2
    assert feat_size == 4
    vmem = pl.BlockSpec(memory_space=pltpu.VMEM)
    smem = pl.BlockSpec(memory_space=pltpu.SMEM)
    slots, cap = local_values.shape[2], remote_values.shape[3]
    lay = Layout(slots, rounds, cap, need, own, part)
    tile_flops = 2 * block * block * feat * lay.tiles
    ints = (local_rows, local_cols, remote_rows, remote_slots, send_blocks, tile_counts)
    meta = jnp.concatenate([a.reshape(-1) for a in ints])
    plan, grad_hidden, degree = pl.pallas_call(
        functools.partial(plan_kernel, lay),
        out_shape=(
            jax.ShapeDtypeStruct((lay.plan_size,), jnp.int32),
            jax.ShapeDtypeStruct((own, block, feat), BF16),
            jax.ShapeDtypeStruct((own, block, block), F32),
        ),
        in_specs=[smem, vmem, vmem, vmem, vmem],
        out_specs=(smem, vmem, vmem),
        scratch_shapes=[pltpu.VMEM((own + 1, block, block), F32)],
        compiler_params=pltpu.CompilerParams(vmem_limit_bytes=VMEM_LIMIT),
        cost_estimate=pl.CostEstimate(
            flops=tile_flops // 2, bytes_accessed=4 * 2**20, transcendentals=0
        ),
        name="plan",
    )(meta, grad_out, weight, local_values, remote_values)
    dma = pltpu.SemaphoreType.DMA
    halves = pltpu.VMEM((rounds, half, block, feat), BF16)
    pairs = (feat_size // 2, own, block, feat)
    output, grad_features = pl.pallas_call(
        functools.partial(exchange_kernel, lay, bits, feat_size),
        out_shape=(
            jax.ShapeDtypeStruct((rows_dev, feat), BF16),
            jax.ShapeDtypeStruct((rows_dev, feat), BF16),
        ),
        in_specs=[smem, smem, vmem, vmem, vmem, vmem, vmem, vmem],
        out_specs=(vmem, vmem),
        scratch_shapes=[
            pltpu.VMEM((part, block, feat), BF16),
            halves,
            halves,
            halves,
            halves,
            halves,
            pltpu.VMEM(pairs, BF16),
            pltpu.VMEM(pairs, BF16),
            pltpu.VMEM(pairs, F32),
            pltpu.VMEM((own, block, feat), BF16),
            pltpu.VMEM((own, block, feat), BF16),
            pltpu.VMEM((rounds * cap, block, feat), F32),
            pltpu.VMEM((slots, block, feat), F32),
            pltpu.VMEM((lay.tiles, block, feat), F32),
            dma((3,)),
            dma((3,)),
            *[dma((rounds,))] * 8,
            dma((2,)),
            dma((2,)),
            *[pltpu.VMEM((need, block, feat), BF16)] * rounds,
        ],
        compiler_params=pltpu.CompilerParams(
            vmem_limit_bytes=VMEM_LIMIT, collective_id=0, has_side_effects=True
        ),
        cost_estimate=pl.CostEstimate(
            flops=2 * tile_flops, bytes_accessed=8 * 2**20, transcendentals=0
        ),
        name="exchange",
    )(meta, plan, features, weight, local_values, remote_values, grad_hidden, degree)
    return (output, grad_features)


def solution(mesh):
    in_specs = (
        P(("node", "feat"), None),
        P(),
        P(("node", "feat"), None),
        P("node", "feat", None),
        P("node", "feat", None),
        P("node", "feat", None, None, None),
        P("node", "feat", None, None),
        P("node", "feat", None, None),
        P("node", "feat", None, None, None, None),
        P("node", None, None),
        P("node", "feat", None),
    )
    out_specs = (P(("node", "feat"), None), P(("node", "feat"), None))
    return jax.shard_map(body, mesh=mesh, in_specs=in_specs, out_specs=out_specs, check_vma=False)
```

time: 89.5 us -> 80 us (0.89)
  Pallas kernels: 84.1 us -> 71.6 us
  other arithmetic: 0 us -> 2.1 us
    pallas_call x3 -> x2, Pallas kernels: 84.1 us -> 71.6 us  [the longest x1 61.7 us: body(): pl.pallas_call(functools.partial(exchange_kernel, lay, bits, feat_size),...]
    unnamed x0 -> x3, other arithmetic: none -> 2.1 us
    concatenate x0 -> x1, local copies, waits for them, and re-layouts: none -> 1.36 us  [body(): meta = jnp.concatenate([a.reshape(-1) for a in ints])]
    unnamed x6 -> x2, local copies, waits for them, and re-layouts: 4.58 us -> 3.74 us
where the time goes in v2:
time: 80 us; the launch traced here: 79.7 us
  Pallas kernels  71.6 us (89%)
  local copies, waits for them, and re-layouts  5.35 us (7%)
  other arithmetic  2.1 us (3%)
    pallas_call x1, Pallas kernels, body(): pl.pallas_call(functools.partial(exchange_kernel, lay, bits, feat_size),...  61.7 us
    pallas_call x1, Pallas kernels, body(): pl.pallas_call(functools.partial(plan_kernel, lay), out_shape=(jax.ShapeD...  9.9 us
    unnamed x2, local copies, waits for them, and re-layouts  3.74 us
    unnamed x3, other arithmetic  2.1 us

profile of v2, /device:TPU:7, one launch (start us, length us, event | category | flops | bytes accessed | tf_op | source)
XLA Modules:
  0.0 79.7 jit_solution(6770223787583797880)
XLA Ops:
  0.6 0.7 reduce
  1.3 0.1 reshape.24
  1.4 0.7 reduce.1
  2.1 0.1 reshape.25
  2.2 0.7 reduce.2
  2.9 0.1 reshape.26
  3.0 1.4 %concatenate.3.meta = s32[212]{0:T(256)} concatenate(s32[32]{0:T(128)} %bitcast.3, s32[32]{0:T(128)} %bitcast.4, s32[48]{0:T(128)S(1)} %reshape.24, s32[48]{0:T(128)S(1)} %reshape.25, s32[48]{0:T(128)S(1)} %reshape.26, s32[4]{0:T(128)} %bitcast.5), dimensions={0} | concatenate | bytes 1696 | tf_op jit(solution)/shard_map/concatenate | solution.py:389
  4.3 9.9 %plan.1 = (s32[344]{0:T(512)}, bf16[8,128,256]{2,1,0:T(8,128)(2,1)}, f32[8,128,128]{2,1,0:T(8,128)}) custom-call(s32[212]{0:T(256)} %concatenate.3.meta, bf16[1024,256]{1,0:T(8,128)(2,1)} %grad_out.1, bf16[256,256]{1,0:T(8,128)(2,1)} %weight.3, bf16[1,1,32,128,128]{4,3,2,1,0:T(8,128)(2,1)} %local_values.3, bf16[1,1,3,16,128,128]{5,4,3,2,1,0:T(8,128)(2,1)} %remote_values.3), custom_call_target="tpu_custom_call" | custom-call | flops 335544320 | bytes 4194304 | tf_op jit(solution)/shard_map/plan/pallas_call | solution.py:390
  14.3 61.7 %exchange.1 = (bf16[1024,256]{1,0:T(8,128)(2,1)}, bf16[1024,256]{1,0:T(8,128)(2,1)}) custom-call(s32[212]{0:T(256)} %concatenate.3.meta, s32[344]{0:T(512)} %get-tuple-element.5.plan, bf16[1024,256]{1,0:T(8,128)(2,1)} %features.1, bf16[256,256]{1,0:T(8,128)(2,1)} %weight.3, bf16[1,1,32,128,128]{4,3,2,1,0:T(8,128)(2,1)} %local_values.3, ...), custom_call_target="tpu_custom_call" | custom-call | flops 1342177280 | bytes 8388608 | tf_op jit(solution)/shard_map/exchange/pallas_call | solution.py:409
  76.0 1.9 %copy.15 = bf16[1024,256]{1,0:T(8,128)(2,1)} copy(bf16[1024,256]{1,0:T(8,128)(2,1)} %get-tuple-element.10) | data formatting | bytes 1048576
  77.9 1.9 %copy.16 = bf16[1024,256]{1,0:T(8,128)(2,1)} copy(bf16[1024,256]{1,0:T(8,128)(2,1)} %get-tuple-element.11) | data formatting | bytes 1048576

commit v3 on v2

--- a/solution.py
+++ b/solution.py
@@ -156,6 +156,9 @@
     back_recv,
     red_send,
     red_recv,
+    far_send,
+    far_recv,
+    far_in,
     *arrived,
 ):
     rounds = len(bits)
@@ -193,6 +196,7 @@
     pair = remote(mine, mine, feat_send.at[1], feat_recv.at[1], to_mate)
     pair.start()
     order = list(range(rounds))[::-1]
+    far, quarter = rounds - 1, half // 2
 
     def picked(sums, at):
         return jnp.where(at >= 0, sums[jnp.maximum(at, 0)], 0.0)
@@ -216,42 +220,99 @@
 
     swaps, backs = [None] * rounds, [None] * rounds
 
+    def slot_of(r, side, i):
+        if r == far:
+            return (2 * (i // quarter) + side) * quarter + lax.rem(i, quarter)
+        return side * half + i
+
+    def swap_with_mate(r):
+        back_products(r)
+
+        @pl.loop(0, half)
+        def _(i):
+            mate_out[r, i] = parcel(r, slot_of(r, mate_h, i)).astype(BF16)
+
+        swaps[r] = remote(
+            mate_out.at[r], mate_parcel.at[r], parcel_send.at[r], parcel_recv.at[r], to_mate
+        )
+        swaps[r].start()
+
+    def paired(r, i):
+        return parcel(r, slot_of(r, h, i)) + mate_parcel[r, i].astype(F32)
+
     def send_back(r):
         swaps[r].wait()
 
         @pl.loop(0, half)
         def _(i):
-            total = parcel(r, h * half + i) + mate_parcel[r, i].astype(F32)
-            parcel_out[r, i] = total.astype(BF16)
+            parcel_out[r, i] = paired(r, i).astype(BF16)
 
         backs[r] = remote(
             parcel_out.at[r], returned.at[r], back_send.at[r], back_recv.at[r], to_node[r]
         )
         backs[r].start()
 
-    for k, r in enumerate(order):
-        back_products(r)
-
-        @pl.loop(0, half)
-        def _(i):
-            mate_out[r, i] = parcel(r, mate_h * half + i).astype(BF16)
-
-        swaps[r] = remote(
-            mate_out.at[r], mate_parcel.at[r], parcel_send.at[r], parcel_recv.at[r], to_mate
-        )
-        swaps[r].start()
-        if k:
-            send_back(order[k - 1])
-    send_back(order[-1])
+    swap_with_mate(far)
+    if far > 0:
+        swap_with_mate(far - 1)
+    swaps[far].wait()
+
+    @pl.loop(0, quarter)
+    def _(i):
+        at = (opp // 2) * quarter + i
+        parcel_out[far, quarter + i] = paired(far, at).astype(BF16)
+
+    far_swap = remote(
+        parcel_out.at[far, pl.ds(quarter, quarter)],
+        far_in,
+        far_send.at[0],
+        far_recv.at[0],
+        to_opp,
+    )
+    far_swap.start()
+    if far > 0:
+        send_back(far - 1)
+    for r in order[2:]:
+        swap_with_mate(r)
+        send_back(r)
 
     cross.wait()
     theirs = part_feats.at[pl.ds(opp * own, own)]
     relay = remote(theirs, theirs, feat_send.at[2], feat_recv.at[2], to_mate)
     relay.start()
+    far_swap.wait()
+
+    @pl.loop(0, quarter)
+    def _(i):
+        total = paired(far, (f // 2) * quarter + i) + far_in[i].astype(F32)
+        parcel_out[far, i] = total.astype(BF16)
+
+    backs[far] = remote(
+        parcel_out.at[far, pl.ds(0, quarter)],
+        returned.at[far, pl.ds(0, quarter)],
+        back_send.at[far],
+        back_recv.at[far],
+        to_node[far],
+    )
+    backs[far].start()
     pair.wait()
     relay.wait()
     outs = [None] * rounds
-    for r in order:
+    my_quarter = arrived[far].at[pl.ds(f * quarter, quarter)]
+
+    @pl.loop(0, quarter)
+    def _(i):
+        send_buf[far, i] = part_feats[meta[lay.send + far * need + f * quarter + i]]
+
+    outs[far] = remote(
+        send_buf.at[far, pl.ds(0, quarter)],
+        my_quarter,
+        node_send.at[far],
+        node_recv.at[far],
+        to_node[far],
+    )
+    outs[far].start()
+    for r in order[1:]:
 
         @pl.loop(0, half)
         def _(i):
@@ -284,9 +345,10 @@
     def gathered_sum(b):
         total = picked(sums_l, plan[lay.last_l + b])
         for r in range(rounds):
-            at = plan[lay.place + r * lay.part + b] - h * half
-            there = jnp.logical_and(at >= 0, at < half)
-            found = returned[r, jnp.clip(at, 0, half - 1)].astype(F32)
+            count, first = (quarter, f * quarter) if r == far else (half, h * half)
+            at = plan[lay.place + r * lay.part + b] - first
+            there = jnp.logical_and(at >= 0, at < count)
+            found = returned[r, jnp.clip(at, 0, count - 1)].astype(F32)
             total = total + jnp.where(there, found, 0.0)
         return total
 
@@ -322,7 +384,8 @@
         passes[r].start()
 
     def forward_products(r):
-        passes[r].wait()
+        if r < far:
+            passes[r].wait()
 
         def step(ts):
             prods = [
@@ -337,18 +400,33 @@
 
         grouped(lay.cap, step)
 
-    for r in range(rounds):
+    def finish_grad():
+        cross_red.wait()
+        for j in range(own):
+            o = f // 2
+            total = kept[o, j] + pair_in[o, j].astype(F32)
+            total = total + cross_in[j].astype(F32) + grad_hidden[j].astype(F32)
+            grad_features[pl.ds(j * block, block), :] = total.astype(BF16)
+
+    outs[far].wait()
+    far_opp = remote(my_quarter, my_quarter, far_send.at[1], far_recv.at[1], to_opp)
+    far_opp.start()
+    far_mate = remote(my_quarter, my_quarter, pass_send.at[far], pass_recv.at[far], to_mate)
+    far_mate.start()
+    for r in range(far):
         pass_on(r)
         if r:
             forward_products(r - 1)
-        if r == rounds - 2:
-            cross_red.wait()
-            for j in range(own):
-                o = f // 2
-                total = kept[o, j] + pair_in[o, j].astype(F32)
-                total = total + cross_in[j].astype(F32) + grad_hidden[j].astype(F32)
-                grad_features[pl.ds(j * block, block), :] = total.astype(BF16)
-    forward_products(rounds - 1)
+    finish_grad()
+    far_opp.wait()
+    opp_quarter = arrived[far].at[pl.ds(opp * quarter, quarter)]
+    far_relay = remote(opp_quarter, opp_quarter, far_send.at[2], far_recv.at[2], to_mate)
+    far_relay.start()
+    if far > 0:
+        forward_products(far - 1)
+    far_mate.wait()
+    far_relay.wait()
+    forward_products(far)
     for d in range(own):
         rows = pl.ds(d * block, block)
         total = features[rows, :].astype(F32) + picked(sums_f, plan[lay.last_f + d])
@@ -434,6 +512,9 @@
             *[dma((rounds,))] * 8,
             dma((2,)),
             dma((2,)),
+            dma((3,)),
+            dma((3,)),
+            pltpu.VMEM((half // 2, block, feat), BF16),
             *[pltpu.VMEM((need, block, feat), BF16)] * rounds,
         ],
         compiler_params=pltpu.CompilerParams(

time: 80 us -> 88.2 us (1.10); the launches traced: 79.7 us -> 86.9 us
  Pallas kernels: 71.6 us -> 78.8 us
    pallas_call x1, Pallas kernels: 61.7 us -> 68.8 us  [body(): pl.pallas_call(functools.partial(exchange_kernel, lay, bits, feat_size),...]
where the time goes in v3:
time: 88.2 us; the launch traced here: 86.9 us
  Pallas kernels  78.8 us (89%)
  local copies, waits for them, and re-layouts  5.35 us (6%)
  other arithmetic  2.1 us (2%)
    pallas_call x1, Pallas kernels, body(): pl.pallas_call(functools.partial(exchange_kernel, lay, bits, feat_size),...  68.8 us
    pallas_call x1, Pallas kernels, body(): pl.pallas_call(functools.partial(plan_kernel, lay), out_shape=(jax.ShapeD...  10 us
    unnamed x2, local copies, waits for them, and re-layouts  3.74 us
    unnamed x3, other arithmetic  2.1 us

profile of v3, /device:TPU:7, one launch (start us, length us, event | category | flops | bytes accessed | tf_op | source)
XLA Modules:
  0.0 86.9 jit_solution(3150114157902936201)
XLA Ops:
  0.6 0.7 reduce
  1.3 0.1 reshape.24
  1.4 0.7 reduce.1
  2.1 0.1 reshape.25
  2.2 0.7 reduce.2
  2.9 0.1 reshape.26
  3.0 1.4 %concatenate.3.meta = s32[212]{0:T(256)} concatenate(s32[32]{0:T(128)} %bitcast.3, s32[32]{0:T(128)} %bitcast.4, s32[48]{0:T(128)S(1)} %reshape.24, s32[48]{0:T(128)S(1)} %reshape.25, s32[48]{0:T(128)S(1)} %reshape.26, s32[4]{0:T(128)} %bitcast.5), dimensions={0} | concatenate | bytes 1696 | tf_op jit(solution)/shard_map/concatenate | solution.py:467
  4.3 10.0 %plan.1 = (s32[344]{0:T(512)}, bf16[8,128,256]{2,1,0:T(8,128)(2,1)}, f32[8,128,128]{2,1,0:T(8,128)}) custom-call(s32[212]{0:T(256)} %concatenate.3.meta, bf16[1024,256]{1,0:T(8,128)(2,1)} %grad_out.1, bf16[256,256]{1,0:T(8,128)(2,1)} %weight.3, bf16[1,1,32,128,128]{4,3,2,1,0:T(8,128)(2,1)} %local_values.3, bf16[1,1,3,16,128,128]{5,4,3,2,1,0:T(8,128)(2,1)} %remote_values.3), custom_call_target="tpu_custom_call" | custom-call | flops 335544320 | bytes 4194304 | tf_op jit(solution)/shard_map/plan/pallas_call | solution.py:468
  14.4 68.8 %exchange.1 = (bf16[1024,256]{1,0:T(8,128)(2,1)}, bf16[1024,256]{1,0:T(8,128)(2,1)}) custom-call(s32[212]{0:T(256)} %concatenate.3.meta, s32[344]{0:T(512)} %get-tuple-element.5.plan, bf16[1024,256]{1,0:T(8,128)(2,1)} %features.1, bf16[256,256]{1,0:T(8,128)(2,1)} %weight.3, bf16[1,1,32,128,128]{4,3,2,1,0:T(8,128)(2,1)} %local_values.3, ...), custom_call_target="tpu_custom_call" | custom-call | flops 1342177280 | bytes 8388608 | tf_op jit(solution)/shard_map/exchange/pallas_call | solution.py:487
  83.1 1.9 %copy.15 = bf16[1024,256]{1,0:T(8,128)(2,1)} copy(bf16[1024,256]{1,0:T(8,128)(2,1)} %get-tuple-element.10) | data formatting | bytes 1048576
  85.0 1.9 %copy.16 = bf16[1024,256]{1,0:T(8,128)(2,1)} copy(bf16[1024,256]{1,0:T(8,128)(2,1)} %get-tuple-element.11) | data formatting | bytes 1048576

commit v4 on v2

--- a/solution.py
+++ b/solution.py
@@ -55,8 +55,12 @@
     block = local_values.shape[-1]
     feat = grad_out.shape[1]
 
-    @pl.loop(0, lay.plan_size)
+    @pl.loop(0, lay.plan_size // GROUP)
     def _(i):
+        for u in range(GROUP):
+            plan[i * GROUP + u] = -1
+
+    for i in range(lay.plan_size // GROUP * GROUP, lay.plan_size):
         plan[i] = -1
 
     @pl.loop(0, lay.slots)
@@ -123,12 +127,11 @@
     meta,
     plan,
     features,
-    weight,
     local_values,
     remote_values,
     grad_hidden,
     degree,
-    output,
+    hidden,
     grad_features,
     part_feats,
     send_buf,
@@ -353,8 +356,7 @@
         rows = pl.ds(d * block, block)
         total = features[rows, :].astype(F32) + picked(sums_f, plan[lay.last_f + d])
         wide = jnp.concatenate([degree[d]] * (feat // block), axis=1)
-        hidden = (total / wide).astype(BF16)
-        output[rows, :] = dot(hidden, weight[...]).astype(BF16)
+        hidden[rows, :] = (total / wide).astype(BF16)
 
 
 def body(
@@ -406,13 +408,13 @@
     dma = pltpu.SemaphoreType.DMA
     halves = pltpu.VMEM((rounds, half, block, feat), BF16)
     pairs = (feat_size // 2, own, block, feat)
-    output, grad_features = pl.pallas_call(
+    hidden, grad_features = pl.pallas_call(
         functools.partial(exchange_kernel, lay, bits, feat_size),
         out_shape=(
             jax.ShapeDtypeStruct((rows_dev, feat), BF16),
             jax.ShapeDtypeStruct((rows_dev, feat), BF16),
         ),
-        in_specs=[smem, smem, vmem, vmem, vmem, vmem, vmem, vmem],
+        in_specs=[smem, smem, vmem, vmem, vmem, vmem, vmem],
         out_specs=(vmem, vmem),
         scratch_shapes=[
             pltpu.VMEM((part, block, feat), BF16),
@@ -443,7 +445,8 @@
             flops=2 * tile_flops, bytes_accessed=8 * 2**20, transcendentals=0
         ),
         name="exchange",
-    )(meta, plan, features, weight, local_values, remote_values, grad_hidden, degree)
+    )(meta, plan, features, local_values, remote_values, grad_hidden, degree)
+    output = dot(hidden, weight).astype(BF16)
     return (output, grad_features)
 
 

time: 80 us -> 78.4 us (0.980)
  matrix products: 0 us -> 2.14 us
  Pallas kernels: 71.6 us -> 69.7 us
  local copies, waits for them, and re-layouts: 5.35 us -> 3.49 us
    dot_general x0 -> x1, matrix products: none -> 2.14 us  [dot(): return jnp.dot(a, b, preferred_element_type=F32)]
    unnamed x2 -> x3, local copies, waits for them, and re-layouts: 3.74 us -> 1.87 us
    pallas_call x1, Pallas kernels: 9.9 us -> 8.19 us  [body(): pl.pallas_call(functools.partial(plan_kernel, lay), out_shape=(jax.ShapeD...]
where the time goes in v4:
time: 78.4 us; the launch traced here: 78.1 us
  Pallas kernels  69.7 us (89%)
  local copies, waits for them, and re-layouts  3.49 us (4%)
  matrix products  2.14 us (3%)
  other arithmetic  2.1 us (3%)
    pallas_call x1, Pallas kernels, body(): pl.pallas_call(functools.partial(exchange_kernel, lay, bits, feat_size),...  61.5 us
    pallas_call x1, Pallas kernels, body(): pl.pallas_call(functools.partial(plan_kernel, lay), out_shape=(jax.ShapeD...  8.19 us
    dot_general x1, matrix products, dot(): return jnp.dot(a, b, preferred_element_type=F32)  2.14 us
    unnamed x3, other arithmetic  2.1 us
    unnamed x3, local copies, waits for them, and re-layouts  1.87 us

profile of v4, /device:TPU:7, one launch (start us, length us, event | category | flops | bytes accessed | tf_op | source)
XLA Modules:
  0.0 78.1 jit_solution(11460994158453249111)
XLA Ops:
  0.6 0.7 reduce
  1.3 0.1 reshape.24
  1.4 0.7 reduce.1
  2.1 0.1 reshape.25
  2.2 0.7 reduce.2
  2.9 0.1 reshape.26
  3.0 1.4 %concatenate.3.meta = s32[212]{0:T(256)} concatenate(s32[32]{0:T(128)} %bitcast.5, s32[32]{0:T(128)} %bitcast.6, s32[48]{0:T(128)S(1)} %reshape.24, s32[48]{0:T(128)S(1)} %reshape.25, s32[48]{0:T(128)S(1)} %reshape.26, s32[4]{0:T(128)} %bitcast.7), dimensions={0} | concatenate | bytes 1696 | tf_op jit(solution)/shard_map/concatenate | solution.py:391
  4.3 8.2 %plan.1 = (s32[344]{0:T(512)}, bf16[8,128,256]{2,1,0:T(8,128)(2,1)}, f32[8,128,128]{2,1,0:T(8,128)}) custom-call(s32[212]{0:T(256)} %concatenate.3.meta, bf16[1024,256]{1,0:T(8,128)(2,1)} %grad_out.1, bf16[256,256]{1,0:T(8,128)(2,1)} %weight.1, bf16[1,1,32,128,128]{4,3,2,1,0:T(8,128)(2,1)} %local_values.3, bf16[1,1,3,16,128,128]{5,4,3,2,1,0:T(8,128)(2,1)} %remote_values.3), custom_call_target="tpu_custom_call" | custom-call | flops 335544320 | bytes 4194304 | tf_op jit(solution)/shard_map/plan/pallas_call | solution.py:392
  12.6 0.0 copy-start
  12.6 61.5 %exchange.1 = (bf16[1024,256]{1,0:T(8,128)(2,1)}, bf16[1024,256]{1,0:T(8,128)(2,1)}) custom-call(s32[212]{0:T(256)} %concatenate.3.meta, s32[344]{0:T(512)} %get-tuple-element.7.plan, bf16[1024,256]{1,0:T(8,128)(2,1)} %features.1, bf16[1,1,32,128,128]{4,3,2,1,0:T(8,128)(2,1)} %local_values.3, bf16[1,1,3,16,128,128]{5,4,3,2,1,0:T(8,128)(2,1)} %remote_values.3, ...), custom_call_target="tpu_custom_call" | custom-call | flops 1342177280 | bytes 8388608 | tf_op jit(solution)/shard_map/exchange/pallas_call | solution.py:411
  74.1 0.0 copy-done
  74.1 2.1 %convolution_convert_fusion = bf16[1024,256]{1,0:T(8,128)(2,1)} fusion(bf16[1024,256]{1,0:T(8,128)(2,1)} %get-tuple-element.10, bf16[256,256]{1,0:T(8,128)(2,1)S(1)} %copy-done), kind=kOutput, calls=%fused_computation | convolution fusion | flops 134479872 | bytes 1179648 | tf_op jit(solution)/shard_map/dot_general | solution.py:17
  76.3 1.9 %copy.14 = bf16[1024,256]{1,0:T(8,128)(2,1)} copy(bf16[1024,256]{1,0:T(8,128)(2,1)} %get-tuple-element.15) | data formatting | bytes 1048576
Async XLA Ops:
  12.6 61.6 %copy-start = (bf16[256,256]{1,0:T(8,128)(2,1)S(1)}, bf16[256,256]{1,0:T(8,128)(2,1)}, u32[]{:S(2)}) copy-start(bf16[256,256]{1,0:T(8,128)(2,1)} %weight.1) | copy-start | bytes 393220
